TPU v7x, 512 devices: a whole 4x4x16 slice. The times are simulated.
512 devices in a mesh: replica: 16 (over z_hi, x), fsdp: 32 (over y, z_lo, core).
Axes of the slice: x: 4, y: 4, z: 16 (z_hi: 4, z_lo: 4; z = z_hi * 4 + z_lo), core: 2. Of those that a mesh axis runs over, the one named last changes fastest.
Arguments:
- acts: bfloat16 [65536, 8192], P(('replica', 'fsdp')), may hold values from -24 to 24
- norm_gain: float32 [8192], replicated, may hold values from 0.5 to 1.5
- cotangent: bfloat16 [65536, 512], P(('replica', 'fsdp')), may hold values from -0.59765625 to 0.59765625
- inner_weight: float32 [16, 8192, 512], P('replica', 'fsdp'), may hold values from -0.18 to 0.18
- first_moment: bfloat16 [16, 8192, 512], P('replica', 'fsdp'), may hold values from -6 to 6
- second_moment: bfloat16 [16, 8192, 512], P('replica', 'fsdp'), may hold values from 0.049804688 to 5
- local_fragment: float32 [16, 8192, 512], P('replica', 'fsdp'), may hold values from -0.0625 to 0.0625
- global_fragment: float32 [8192, 512], P('fsdp', 'replica'), may hold values from -0.0625 to 0.0625
- outer_momentum: float32 [8192, 512], P('fsdp', 'replica'), may hold values from -0.06 to 0.06
Outputs:
- new_weight: float32 [16, 8192, 512], P('replica', 'fsdp')
- new_first_moment: bfloat16 [16, 8192, 512], P('replica', 'fsdp')
- new_second_moment: bfloat16 [16, 8192, 512], P('replica', 'fsdp')
- new_global: float32 [8192, 512], P('fsdp', 'replica')
- new_momentum: float32 [8192, 512], P('fsdp', 'replica')
- next_features: bfloat16 [65536, 512], P(('replica', 'fsdp'))
All inputs are finite; a program needn't handle non-finite values.
Results may differ from a plain program's by a relative error of at most 0.0058.
Values may be sent and summed in bfloat16 or wider, within the bound.
A program may use at most 64 MiB of HBM per device.

v0:
```python
import jax
import jax.numpy as jnp
from jax import lax
from jax.sharding import PartitionSpec as P

beta_one = 0.9
beta_two = 0.95
adam_epsilon = 1e-08
inner_rate = 0.01
weight_decay = 0.1
bias_first = 1.0 - 0.9**20
bias_second = 1.0 - 0.95**20
outer_rate = 0.7
outer_beta = 0.9
norm_epsilon = 1e-05


def normalize(rows, norm_gain):
    full = rows.astype(jnp.float32)
    rstd = lax.rsqrt(jnp.mean(full * full, axis=1, keepdims=True) + norm_epsilon)
    return (full * rstd * norm_gain[None, :]).astype(jnp.bfloat16)


def inner_step(normed, cotangent, inner_weight, first_moment, second_moment):
    columns = lax.all_to_all(normed, "fsdp", split_axis=1, concat_axis=0, tiled=True)
    every = lax.all_gather(cotangent, "fsdp", axis=0, tiled=True)
    grad = lax.dot_general(
        columns, every, (((0,), (0,)), ((), ())), preferred_element_type=jnp.float32
    )
    grad = grad[None]
    first = beta_one * first_moment.astype(jnp.float32) + (1.0 - beta_one) * grad
    second = beta_two * second_moment.astype(jnp.float32) + (1.0 - beta_two) * grad * grad
    ratio = first / bias_first / (jnp.sqrt(second / bias_second) + adam_epsilon)
    new_weight = inner_weight - inner_rate * (ratio + weight_decay * inner_weight)
    return (new_weight, first.astype(jnp.bfloat16), second.astype(jnp.bfloat16))


def outer_step(normed, local_fragment, global_fragment, outer_momentum):
    total = lax.psum_scatter(local_fragment[0], "replica", scatter_dimension=1, tiled=True)
    mean_delta = global_fragment - total / lax.axis_size("replica")
    new_momentum = outer_beta * outer_momentum + mean_delta
    new_global = global_fragment - outer_rate * (mean_delta + outer_beta * new_momentum)
    narrow = new_global.astype(jnp.bfloat16)
    wide_rows = lax.all_gather(narrow, "replica", axis=1, tiled=True)
    feats = jnp.dot(
        normed,
        lax.all_gather(wide_rows, "fsdp", axis=0, tiled=True),
        preferred_element_type=jnp.float32,
    )
    next_features = feats.astype(jnp.bfloat16)
    return (new_global, new_momentum, next_features)


def body(
    acts,
    norm_gain,
    cotangent,
    inner_weight,
    first_moment,
    second_moment,
    local_fragment,
    global_fragment,
    outer_momentum,
):
    normed = normalize(acts, norm_gain)
    new_weight, new_first, new_second = inner_step(
        normed, cotangent, inner_weight, first_moment, second_moment
    )
    new_global, new_momentum, next_features = outer_step(
        normed, local_fragment, global_fragment, outer_momentum
    )
    return (new_weight, new_first, new_second, new_global, new_momentum, next_features)


def solution(mesh):
    placed = (
        P(("replica", "fsdp"), None),
        P(),
        P(("replica", "fsdp"), None),
        P("replica", "fsdp", None),
        P("replica", "fsdp", None),
        P("replica", "fsdp", None),
        P("replica", "fsdp", None),
        P("fsdp", "replica"),
        P("fsdp", "replica"),
    )
    return jax.shard_map(
        body,
        mesh=mesh,
        in_specs=placed,
        out_specs=(
            P("replica", "fsdp", None),
            P("replica", "fsdp", None),
            P("replica", "fsdp", None),
            P("fsdp", "replica"),
            P("fsdp", "replica"),
            P(("replica", "fsdp"), None),
        ),
        check_vma=False,
    )
```

profile of v0, /device:TPU:24, one launch (start us, length us, event | category | flops | bytes accessed | tf_op | source)
XLA Modules:
  0.0 318.6 jit_solution(13601042559405675904)
XLA Ops:
  8.0 0.0 copy-start.2
  8.0 0.0 reduce-scatter.2.cloned.1.call-start
  8.1 2.0 copy.19
  10.1 0.0 reduce-scatter.2.cloned.1.call-update
  10.1 0.0 all-gather.3.cloned.1.call-start
  10.2 0.5 all-gather.3.cloned.1.call-update
  10.7 0.0 all-gather.5.cloned.1.call-start
  10.7 120.5 %reduce-scatter.2.cloned.1.call-done = f32[256,32]{0,1:T(8,128)} async-done(((f32[256,512]{0,1:T(8,128)}), f32[256,32]{0,1:T(8,128)}) %reduce-scatter.2.cloned.1.call-update) | async-done | bytes 32784 | tf_op jit(solution)/shard_map/reduce_scatter | solution.py:39
  131.3 1.4 fusion.7
  132.7 55.3 %all_gather.10 = bf16[256,512]{0,1:T(8,128)(2,1)} all-gather(bf16[256,32]{0,1:T(8,128)(2,1)S(1)} %get-tuple-element.6), channel_id=1, replica_groups=mesh['replica'=16,'fsdp'=32] {'replica'}, dimensions={1}, use_global_device_ids=true | all-gather | bytes 278528 | tf_op jit(solution)/shard_map/all_gather | solution.py:44
  188.0 0.0 all-gather.5.cloned.1.call-update
  188.1 3.2 %copy.17 = bf16[128,8192]{0,1:T(8,128)(2,1)S(1)} copy(bf16[128,8192]{1,0:T(8,128)(2,1)} %param.9) | data formatting | bytes 4194304 | tf_op args[0]
  191.3 1.1 fusion
  192.4 0.0 copy-done.2
  192.4 3.5 %fusion.2 = bf16[128,8192]{0,1:T(8,128)(2,1)S(1)} fusion(bf16[128,8192]{0,1:T(8,128)(2,1)S(1)} %copy.17, f32[8192]{0:T(1024)S(1)} %copy-done.2, f32[128]{0:T(128)S(1)} %add_rsqrt_fusion), kind=kLoop, calls=%fused_computation.4 | loop fusion | flops 4194304 | bytes 4227584 | tf_op jit(solution)/shard_map/convert_element_type | solution.py:21
  195.9 0.0 copy-start
  195.9 1.3 copy-done
  197.2 0.0 copy-start.3
  197.2 0.0 copy-start.4
  197.2 0.0 copy-start.5
  197.2 65.8 %all_to_all.19 = bf16[128,32,256]{0,2,1:T(8,128)(2,1)S(1)} all-to-all(bf16[128,32,256]{0,2,1:T(8,128)(2,1)S(1)} %bitcast.22), channel_id=1, replica_groups=mesh['replica'=16,'fsdp'=32] {'fsdp'}, dimensions={1} | all-to-all | bytes 4194304 | tf_op jit(solution)/shard_map/all_to_all | solution.py:25
  263.1 2.9 copy.18
  265.9 0.0 all-gather.3.cloned.1.call-done
  266.0 0.0 copy-done.3
  266.0 0.0 copy-done.4
  266.0 0.0 copy-done.5
  266.0 0.0 copy-start.1
  266.0 5.7 %fusion.6 = (bf16[1,256,512]{2,1,0:T(8,128)(2,1)}, f32[1,256,512]{2,1,0:T(8,128)}, bf16[1,256,512]{2,1,0:T(8,128)(2,1)}) fusion(bf16[1,256,512]{2,1,0:T(8,128)(2,1)S(1)} %copy-done.4, f32[1,256,512]{2,1,0:T(8,128)S(1)} %copy-done.3, bf16[1,256,512]{2,1,0:T(8,128)(2,1)S(1)} %copy-done.5, bf16[4096,256]{1,0:T(8,128)(2,1)} %bitcast.24, ...), kind=kOutput, calls=%fused_computation.12 | convolution fusion | flops 1076232192 | bytes 8388608 | tf_op jit(solution)/shard_map/dot_general | solution.py:27
  271.7 32.6 %all-gather.5.cloned.1.call-done = bf16[8192,512]{0,1:T(8,128)(2,1)} async-done(((bf16[256,512]{0,1:T(8,128)(2,1)}), bf16[8192,512]{0,1:T(8,128)(2,1)}) %all-gather.5.cloned.1.call-update) | async-done | bytes 8388624 | tf_op jit(solution)/shard_map/all_gather | solution.py:47
  304.3 0.0 copy-done.1
  304.3 6.9 %convolution_convert_fusion = bf16[128,512]{1,0:T(8,128)(2,1)} fusion(bf16[128,8192]{0,1:T(8,128)(2,1)S(1)} %copy-done.1, bf16[8192,512]{0,1:T(8,128)(2,1)} %all-gather.5.cloned.1.call-done), kind=kOutput, calls=%fused_computation.5 | convolution fusion | flops 1073807360 | bytes 10616832 | tf_op jit(solution)/shard_map/dot_general | solution.py:45
  (1 shorter events, 0.0 us)
Async XLA Ops:
  8.0 184.4 %copy-start.2 = (f32[8192]{0:T(1024)S(1)}, f32[8192]{0:T(1024)}, u32[]{:S(2)}) copy-start(f32[8192]{0:T(1024)} %param.10) | copy-start | bytes 98308
  8.0 123.3 %reduce-scatter.2.cloned.1.call-start = ((), (), s32[]{:S(2)}) async-start(), calls=%async_computation.3 | async-start | bytes 557056 | tf_op jit(solution)/shard_map/reduce_scatter | solution.py:39
  10.1 255.8 %all-gather.3.cloned.1.call-start = ((), (), s32[]{:S(2)}) async-start(), calls=%async_computation.2 | async-start | bytes 4325376 | tf_op jit(solution)/shard_map/all_gather | solution.py:26
  10.7 293.6 %all-gather.5.cloned.1.call-start = ((), (), s32[]{:S(2)}) async-start(), calls=%async_computation.4 | async-start | bytes 8650752 | tf_op jit(solution)/shard_map/all_gather | solution.py:47
  195.9 1.3 copy-start
  197.2 68.7 %copy-start.3 = (f32[1,256,512]{2,1,0:T(8,128)S(1)}, f32[1,256,512]{2,1,0:T(8,128)}, u32[]{:S(2)}) copy-start(f32[1,256,512]{2,1,0:T(8,128)} %param.12) | copy-start | bytes 1572868
  197.2 68.7 %copy-start.4 = (bf16[1,256,512]{2,1,0:T(8,128)(2,1)S(1)}, bf16[1,256,512]{2,1,0:T(8,128)(2,1)}, u32[]{:S(2)}) copy-start(bf16[1,256,512]{2,1,0:T(8,128)(2,1)} %param.14) | copy-start | bytes 786436
  197.2 68.7 %copy-start.5 = (bf16[1,256,512]{2,1,0:T(8,128)(2,1)S(1)}, bf16[1,256,512]{2,1,0:T(8,128)(2,1)}, u32[]{:S(2)}) copy-start(bf16[1,256,512]{2,1,0:T(8,128)(2,1)} %param.13) | copy-start | bytes 786436
  266.0 38.3 %copy-start.1 = (bf16[128,8192]{0,1:T(8,128)(2,1)S(1)}, bf16[128,8192]{0,1:T(8,128)(2,1)}, u32[]{:S(2)}) copy-start(bf16[128,8192]{0,1:T(8,128)(2,1)} %copy-done) | copy-start | bytes 6291460
Sparse Core Ops, SparseCore 0:
  13.5 117.7 reduce-scatter.1
Sparse Core Ops, SparseCore 1:
  12.7 72.3 all-gather.2
  188.1 116.1 all-gather.4
where the time goes:
time: 322 us; the launch traced here: 319 us
  waiting for transfers between devices  154 us (48%)
  blocking collectives  121 us (38%)
  between operations  15.5 us (5%)
  matrix products  12.7 us (4%)
  local copies, waits for them, and re-layouts  9.47 us (3%)
  other arithmetic  6.01 us (2%)
    reduce_scatter x1, waiting for transfers between devices, outer_step(): lax.psum_scatter(local_fragment[0], 'replica', scatter_dimension=1, tiled...  121 us
    all_to_all x1, blocking collectives, inner_step(): lax.all_to_all(normed, 'fsdp', split_axis=1, concat_axis=0, tiled=True)  65.8 us
    all_gather x1, blocking collectives, outer_step(): wide_rows = lax.all_gather(narrow, 'replica', axis=1, tiled=True)  55.3 us
    all_gather x1, waiting for transfers between devices, outer_step(): lax.all_gather(wide_rows, 'fsdp', axis=0, tiled=True)  32.6 us
    dot_general x1, matrix products, outer_step(): jnp.dot(normed, lax.all_gather(wide_rows, 'fsdp', axis=0, tiled=True), pr...  6.94 us
    unnamed x14, local copies, waits for them, and re-layouts  6.6 us
  transfers between devices with their start and end apart: 3, of which 2 were waited for; matrix products, arithmetic and copies ran while one was open for 6% of the time, Pallas kernels for 0%

commit v1 on v0

v1 whole, which is shorter than its diff:
```python
import functools

import jax
import jax.numpy as jnp
from jax import lax
from jax.experimental import pallas as pl
from jax.experimental.pallas import tpu as pltpu
from jax.sharding import PartitionSpec as P

beta_one = 0.9
beta_two = 0.95
adam_epsilon = 1e-08
inner_rate = 0.01
weight_decay = 0.1
bias_first = 1.0 - 0.9**20
bias_second = 1.0 - 0.95**20
outer_rate = 0.7
outer_beta = 0.9
norm_epsilon = 1e-05

MESH = pl.DeviceIdType.MESH
F32 = jnp.float32
BF16 = jnp.bfloat16


def kernel(
    acts_h, gain_h, cot_h, w_h, fm_h, sm_h, lf_h, g_h, m_h,
    w_o, fm_o, sm_o, ng_o, nm_o, ft_o,
    acts, gain, normed, cot, w, fm, sm, lf, g, m,
    lt, lr, part, pr, nt, xs, gsend, gown, grecv, zsend, zrecv, fsend, frecv,
    lsem, xsem, csem_s, csem_r, asem_s, asem_r,
    lsem_s, lsem_r, psem_s, psem_r, hsem_s, hsem_r,
    t2sem_s, t2sem_r, t3sem_s, t3sem_r, dsem_s, dsem_r,
    gsem_s, gsem_r, zsem_s, zsem_r, fsem_s, fsem_r,
):
    rep = lax.axis_index("replica")
    fs = lax.axis_index("fsdp")
    zh, x = rep // 4, lax.rem(rep, 4)
    y, zl, c = fs // 8, lax.rem(fs // 2, 4), lax.rem(fs, 2)
    z = zh * 4 + zl

    def at(zh=zh, x=x, y=y, zl=zl, c=c):
        return (zh * 4 + x, y * 8 + zl * 2 + c)

    def at_z(zz):
        return at(zh=zz // 4, zl=lax.rem(zz, 4))

    def turn(value, step, size):
        return lax.rem(value + step + size, size)

    def send(src, dst, ss, rs, device):
        copy = pltpu.make_async_remote_copy(
            src_ref=src, dst_ref=dst, send_sem=ss, recv_sem=rs,
            device_id=device, device_id_type=MESH,
        )
        copy.start()
        return copy

    other = at(c=1 - c)
    skew = 2 - 4 * lax.rem(zl, 2)
    flips = (3 - zl, lax.rem(zl + 2, 4), zl + 1 - 2 * lax.rem(zl, 2), zl)

    loads = []
    for i, (src, dst) in enumerate((
        (lf_h, lf), (acts_h, acts), (gain_h, gain),
        (cot_h, cot.at[pl.ds(pl.multiple_of(y * 128, 128), 128)]),
        (g_h, g), (m_h, m), (w_h, w), (fm_h, fm), (sm_h, sm),
    )):
        copy = pltpu.make_async_copy(src, dst, lsem.at[i])
        copy.start()
        loads.append(copy)

    barrier = pltpu.get_barrier_semaphore()
    sources = [other]
    sources += [at(y=turn(y, d, 4)) for d in (1, 2, 3)]
    sources += [at(x=turn(x, d, 4)) for d in (1, 2, 3)]
    sources += [at(zh=turn(zh, d, 4)) for d in (1, 2, 3)]
    sources += [at(zl=flips[s]) for s in range(3)]
    sources += [at_z(turn(z, 1, 16)), at_z(turn(z, -1, 16)), at_z(turn(z, -skew, 16))]
    for device in sources:
        pl.semaphore_signal(barrier, inc=1, device_id=device, device_id_type=MESH)

    loads[0].wait()
    for k in range(4):
        turned = lf[:, k * 128:(k + 1) * 128].T
        for j in range(4):
            lt[j, k] = turned[j * 32:(j + 1) * 32]

    loads[1].wait()
    loads[2].wait()

    def norm_rows(i, carry):
        rows = pl.ds(pl.multiple_of(i * 16, 16), 16)
        full = acts[rows, :].astype(F32)
        rstd = lax.rsqrt(jnp.sum(full * full, axis=1, keepdims=True) / 8192.0 + norm_epsilon)
        normed[rows, :] = (full * rstd * gain[...]).astype(BF16)
        return carry

    lax.fori_loop(0, 8, norm_rows, 0)
    loads[3].wait()

    pl.semaphore_wait(barrier, len(sources))

    sends = []
    for i, d in enumerate((1, 3, 2)):
        to = turn(x, d, 4)
        sends.append(send(lt.at[to], lr.at[i], lsem_s.at[i], lsem_r.at[i], at(x=to)))
    along_x = sends[-3:]
    mine = pl.ds(pl.multiple_of(y * 128, 128), 128)
    for i, d in enumerate((1, 3, 2)):
        sends.append(send(cot.at[mine], cot.at[mine], csem_s.at[i], csem_r.at[i], at(y=turn(y, d, 4))))
    cots = sends[-3:]
    chunks, keeps = [], []
    for s in range(4):
        row = []
        for i, d in enumerate((1, 3, 2)):
            to = turn(y, d, 4)
            cols = pl.ds(pl.multiple_of(to * 2048 + flips[s] * 512, 512), 512)
            row.append(send(normed.at[:, cols], xs.at[s, mine], asem_s.at[s * 3 + i], asem_r.at[s * 3 + i], at(y=to)))
        cols = pl.ds(pl.multiple_of(y * 2048 + flips[s] * 512, 512), 512)
        keep = pltpu.make_async_copy(normed.at[:, cols], xs.at[s, mine], xsem.at[s])
        keep.start()
        keeps.append(keep)
        chunks.append(row)
        sends += row

    def sum_x():
        for copy in along_x:
            copy.wait_recv()
        part[...] = lt[x] + lr[0] + lr[1] + lr[2]
        out = []
        for i, d in enumerate((1, 3, 2)):
            to = turn(zh, d, 4)
            out.append(send(part.at[to], pr.at[i], psem_s.at[i], psem_r.at[i], at(zh=to)))
        return out

    def outer_update(copies):
        for copy in copies:
            copy.wait_recv()
        loads[4].wait()
        loads[5].wait()
        total = part[zh] + pr[0] + pr[1] + pr[2]
        mean_delta = g[...] - total / 16.0
        new_momentum = outer_beta * m[...] + mean_delta
        new_global = g[...] - outer_rate * (mean_delta + outer_beta * new_momentum)
        ng_o[...] = new_global
        nm_o[...] = new_momentum
        nt[zl, c, zh, x] = new_global.astype(BF16)
        out = []
        for i, d in enumerate((1, 3, 2)):
            piece = nt.at[zl, c, zh, x]
            out.append(send(piece, piece, hsem_s.at[i], hsem_r.at[i], at(zh=turn(zh, d, 4))))
        return out

    x_peers = [at(x=turn(x, d, 4)) for d in (1, 3, 2)]
    z_peers = [at_z(turn(z, 1, 16)), at_z(turn(z, -1, 16)), at_z(turn(z, skew, 16))]

    def gather_two(copies):
        for copy in copies:
            copy.wait_recv()
        out = []
        for i in range(3):
            piece = nt.at[zl, c, pl.ds(0, 2), x]
            out.append(send(piece, piece, t2sem_s.at[i], t2sem_r.at[i], x_peers[i]))
            piece = nt.at[zl, c, pl.ds(2, 2), x]
            out.append(send(piece, piece, t2sem_s.at[3 + i], t2sem_r.at[3 + i], z_peers[i]))
        return out

    def gather_three(copies):
        for copy in copies:
            copy.wait_recv()
        out = []
        for i in range(3):
            piece = nt.at[zl, c, pl.ds(0, 2)]
            out.append(send(piece, piece, t3sem_s.at[i], t3sem_r.at[i], z_peers[i]))
            piece = nt.at[:, c, pl.ds(2, 2), x]
            out.append(send(piece, piece, t3sem_s.at[3 + i], t3sem_r.at[3 + i], x_peers[i]))
        return out

    def gather_core(copies):
        for copy in copies:
            copy.wait_recv()
        piece = nt.at[:, c]
        return [send(piece, piece, dsem_s.at[0], dsem_r.at[0], other)]

    def half(core):
        return pl.ds(pl.multiple_of(core * 256, 256), 256)

    def grad_of(s, core):
        return lax.dot_general(
            xs[s, :, half(core)], cot[...], (((0,), (0,)), ((), ())), preferred_element_type=F32
        )

    def chunk_in(s):
        for copy in chunks[s]:
            copy.wait_recv()
        keeps[s].wait()
        gsend[s] = grad_of(s, 1 - c)
        copy = send(gsend.at[s], grecv.at[s], gsem_s.at[s], gsem_r.at[s], other)
        gown[s] = grad_of(s, c)
        return copy

    def chunk_out(s, copy):
        copy.wait_recv()
        zsend[s] = (gown[s] + grecv[s]).astype(BF16)
        return send(zsend.at[s], zrecv.at[s], zsem_s.at[s], zsem_r.at[s], at(zl=flips[s]))

    def feature_part(core):
        total = None
        for s in range(4):
            rows = nt[flips[s], core].reshape(512, 256)
            term = lax.dot_general(
                xs[s, :, half(core)], rows, (((1,), (1,)), ((), ())), preferred_element_type=F32
            )
            total = term if total is None else total + term
        return total

    pcopies = sum_x()
    for copy in cots:
        copy.wait_recv()
    hcopies = outer_update(pcopies)
    g0 = chunk_in(0)
    t2 = gather_two(hcopies)
    z0 = chunk_out(0, g0)
    g1 = chunk_in(1)
    t3 = gather_three(t2)
    z1 = chunk_out(1, g1)
    g2 = chunk_in(2)
    z2 = chunk_out(2, g2)
    dcopies = gather_core(t3)
    g3 = chunk_in(3)
    fpart = feature_part(c)
    for copy in dcopies:
        copy.wait_recv()
    fpart = fpart + feature_part(1 - c)
    for k in range(4):
        fsend[k] = fpart[k * 128:(k + 1) * 128]
    fb = frecv.at[3]
    fcopies = []
    for i, d in enumerate((1, 3, 2)):
        to = turn(y, d, 4)
        frecv[4 + i] = fsend[to].astype(BF16)
        fcopies.append(send(frecv.at[4 + i], frecv.at[i], fsem_s.at[i], fsem_r.at[i], at(y=to)))

    g3.wait_recv()
    for i in (6, 7, 8):
        loads[i].wait()
    for copy in (z0, z1, z2):
        copy.wait_recv()
    grad = gown[3] + grecv[3] + zrecv[0].astype(F32) + zrecv[1].astype(F32) + zrecv[2].astype(F32)
    first = beta_one * fm[...].astype(F32) + (1.0 - beta_one) * grad
    second = beta_two * sm[...].astype(F32) + (1.0 - beta_two) * grad * grad
    ratio = first / bias_first / (jnp.sqrt(second / bias_second) + adam_epsilon)
    w_o[...] = w[...] - inner_rate * (ratio + weight_decay * w[...])
    fm_o[...] = first.astype(BF16)
    sm_o[...] = second.astype(BF16)

    for copy in fcopies:
        copy.wait_recv()
    ft_o[...] = (
        fsend[y] + frecv[0].astype(F32) + frecv[1].astype(F32) + frecv[2].astype(F32)
    ).astype(BF16)

    for copy in sends + pcopies + hcopies + t2 + t3 + dcopies + [g0, g1, g2, g3, z0, z1, z2] + fcopies:
        copy.wait_send()


def body(
    acts,
    norm_gain,
    cotangent,
    inner_weight,
    first_moment,
    second_moment,
    local_fragment,
    global_fragment,
    outer_momentum,
):
    vmem, anywhere = pl.BlockSpec(memory_space=pltpu.VMEM), pl.BlockSpec(memory_space=pl.ANY)
    dma = pltpu.SemaphoreType.DMA
    outs = pl.pallas_call(
        kernel,
        out_shape=(
            jax.ShapeDtypeStruct((256, 512), F32),
            jax.ShapeDtypeStruct((256, 512), BF16),
            jax.ShapeDtypeStruct((256, 512), BF16),
            jax.ShapeDtypeStruct((32, 256), F32),
            jax.ShapeDtypeStruct((32, 256), F32),
            jax.ShapeDtypeStruct((128, 512), BF16),
        ),
        in_specs=[anywhere] * 9,
        out_specs=[vmem] * 6,
        scratch_shapes=[
            pltpu.VMEM((128, 8192), BF16),
            pltpu.VMEM((1, 8192), F32),
            pltpu.VMEM((128, 8192), BF16),
            pltpu.VMEM((512, 512), BF16),
            pltpu.VMEM((256, 512), F32),
            pltpu.VMEM((256, 512), BF16),
            pltpu.VMEM((256, 512), BF16),
            pltpu.VMEM((256, 512), F32),
            pltpu.VMEM((32, 256), F32),
            pltpu.VMEM((32, 256), F32),
            pltpu.VMEM((4, 4, 32, 256), F32),
            pltpu.VMEM((3, 4, 32, 256), F32),
            pltpu.VMEM((4, 32, 256), F32),
            pltpu.VMEM((3, 32, 256), F32),
            pltpu.VMEM((4, 2, 4, 4, 32, 256), BF16),
            pltpu.VMEM((4, 512, 512), BF16),
            pltpu.VMEM((4, 256, 512), F32),
            pltpu.VMEM((4, 256, 512), F32),
            pltpu.VMEM((4, 256, 512), F32),
            pltpu.VMEM((3, 256, 512), BF16),
            pltpu.VMEM((3, 256, 512), BF16),
            pltpu.VMEM((4, 128, 512), F32),
            pltpu.VMEM((7, 128, 512), BF16),
            dma((9,)), dma((4,)), dma((3,)), dma((3,)), dma((12,)), dma((12,)),
            dma((3,)), dma((3,)), dma((3,)), dma((3,)), dma((3,)), dma((3,)),
            dma((6,)), dma((6,)), dma((6,)), dma((6,)), dma((1,)), dma((1,)),
            dma((4,)), dma((4,)), dma((3,)), dma((3,)), dma((3,)), dma((3,)),
        ],
        compiler_params=pltpu.CompilerParams(
            collective_id=0, has_side_effects=True, vmem_limit_bytes=63 * 2**20
        ),
        name="window_step",
    )(
        acts, norm_gain[None], cotangent, inner_weight[0], first_moment[0], second_moment[0],
        local_fragment[0], global_fragment.T, outer_momentum.T,
    )
    new_weight, new_first, new_second, new_global, new_momentum, features = outs
    return (new_weight[None], new_first[None], new_second[None], new_global.T, new_momentum.T, features)


def solution(mesh):
    placed = (
        P(("replica", "fsdp"), None),
        P(),
        P(("replica", "fsdp"), None),
        P("replica", "fsdp", None),
        P("replica", "fsdp", None),
        P("replica", "fsdp", None),
        P("replica", "fsdp", None),
        P("fsdp", "replica"),
        P("fsdp", "replica"),
    )
    return jax.shard_map(
        body,
        mesh=mesh,
        in_specs=placed,
        out_specs=(
            P("replica", "fsdp", None),
            P("replica", "fsdp", None),
            P("replica", "fsdp", None),
            P("fsdp", "replica"),
            P("fsdp", "replica"),
            P(("replica", "fsdp"), None),
        ),
        check_vma=False,
    )
```

time: 322 us -> 87.1 us (0.27)
  the two profiles are of different devices: /device:TPU:24 before, /device:TPU:33 now
where the time goes in v1:
time: 87.1 us; the launch traced here: 86.9 us
  Pallas kernels  79.1 us (91%)
  local copies, waits for them, and re-layouts  7.14 us (8%)
    pallas_call x1, Pallas kernels, body(): pl.pallas_call(kernel, out_shape=(jax.ShapeDtypeStruct((256, 512), F32),...  79.1 us
    unnamed x12, local copies, waits for them, and re-layouts  7.14 us

profile of v1, /device:TPU:33, one launch (start us, length us, event | category | flops | bytes accessed | tf_op | source)
XLA Modules:
  0.0 86.9 jit_solution(1035221653526850324)
XLA Ops:
  0.6 79.1 %window_step.1 = (f32[256,512]{1,0:T(8,128)}, bf16[256,512]{1,0:T(8,128)(2,1)}, bf16[256,512]{1,0:T(8,128)(2,1)}, f32[32,256]{1,0:T(8,128)}, f32[32,256]{1,0:T(8,128)}, /*index=5*/bf16[128,512]{1,0:T(8,128)(2,1)}) custom-call(bf16[128,8192]{1,0:T(8,128)(2,1)} %acts_h.1, f32[1,8192]{1,0:T(1,128)} %bitcast.19, bf16[128,512]{1,0:T(8,128)(2,1)} %cot_h.1, ...), custom_call_target="tpu_custom_call" | custom-call | tf_op jit(solution)/shard_map/window_step/pallas_call | solution.py:281
  79.7 0.0 copy-start.2
  79.7 0.0 copy-start.1
  79.7 0.0 copy-start
  79.7 1.9 %copy.21 = f32[1,256,512]{2,1,0:T(8,128)} copy(f32[1,256,512]{2,1,0:T(8,128)} %bitcast.12) | data formatting | bytes 1048576
  81.6 1.7 %copy.22 = bf16[1,256,512]{2,1,0:T(8,128)(2,1)} copy(bf16[1,256,512]{2,1,0:T(8,128)(2,1)} %bitcast.16) | data formatting | bytes 524288
  83.3 1.7 %copy.23 = bf16[1,256,512]{2,1,0:T(8,128)(2,1)} copy(bf16[1,256,512]{2,1,0:T(8,128)(2,1)} %bitcast.15) | data formatting | bytes 524288
  85.0 0.0 copy-done.2
  85.0 0.6 copy.24
  85.6 0.0 copy-done.1
  85.6 0.6 copy.25
  86.2 0.0 copy-done
  86.2 0.7 copy.26
Async XLA Ops:
  79.7 5.3 %copy-start.2 = (f32[32,256]{1,0:T(8,128)S(1)}, f32[32,256]{1,0:T(8,128)}, u32[]{:S(2)}) copy-start(f32[32,256]{1,0:T(8,128)} %get-tuple-element.15) | copy-start | bytes 98308
  79.7 5.9 %copy-start.1 = (f32[32,256]{1,0:T(8,128)S(1)}, f32[32,256]{1,0:T(8,128)}, u32[]{:S(2)}) copy-start(f32[32,256]{1,0:T(8,128)} %get-tuple-element.16) | copy-start | bytes 98308
  79.7 6.5 %copy-start = (bf16[128,512]{1,0:T(8,128)(2,1)S(1)}, bf16[128,512]{1,0:T(8,128)(2,1)}, u32[]{:S(2)}) copy-start(bf16[128,512]{1,0:T(8,128)(2,1)} %get-tuple-element.29) | copy-start | bytes 393220

commit v2 on v1

v2 whole, which is shorter than its diff:
```python
import functools

import jax
import jax.numpy as jnp
from jax import lax
from jax.experimental import pallas as pl
from jax.experimental.pallas import tpu as pltpu
from jax.sharding import PartitionSpec as P

beta_one = 0.9
beta_two = 0.95
adam_epsilon = 1e-08
inner_rate = 0.01
weight_decay = 0.1
bias_first = 1.0 - 0.9**20
bias_second = 1.0 - 0.95**20
outer_rate = 0.7
outer_beta = 0.9
norm_epsilon = 1e-05

MESH = pl.DeviceIdType.MESH
F32 = jnp.float32
BF16 = jnp.bfloat16


def kernel(
    acts_h, gain_h, cot_h, w_h, fm_h, sm_h, lf_h, g_h, m_h,
    w_o, fm_o, sm_o, ng_o, nm_o, ft_o,
    acts, gain, normed, cot, w, fm, sm, lf, g, m,
    lt, lr, part, pr, nt, xs, gsend, gown, grecv, zsend, zrecv, fown, fsend, frecv,
    load_sem, keep_sem, vouch,
    cot_s, cot_r, tok_s, tok_r, along_s, along_r, far_s, far_r, gat_s, gat_r,
    line_s, line_r, wide_s, wide_r, core_s, core_r,
    grad_s, grad_r, z_s, z_r, feat_s, feat_r,
):
    rep = lax.axis_index("replica")
    fs = lax.axis_index("fsdp")
    zh, x = rep // 4, lax.rem(rep, 4)
    y, zl, c = fs // 8, lax.rem(fs // 2, 4), lax.rem(fs, 2)
    z = zh * 4 + zl

    def at(zh=zh, x=x, y=y, zl=zl, c=c):
        return (zh * 4 + x, y * 8 + zl * 2 + c)

    def at_z(zz):
        return at(zh=zz // 4, zl=lax.rem(zz, 4))

    def turn(value, step, size=4):
        return lax.rem(value + step + size, size)

    sends = []

    def send(src, dst, ss, rs, device):
        copy = pltpu.make_async_remote_copy(
            src_ref=src, dst_ref=dst, send_sem=ss, recv_sem=rs,
            device_id=device, device_id_type=MESH,
        )
        copy.start()
        sends.append(copy)
        return copy

    def signal(sem, device):
        pl.semaphore_signal(sem, inc=1, device_id=device, device_id_type=MESH)

    other = at(c=1 - c)
    steps = (1, 3, 2)
    x_peers = [at(x=turn(x, d)) for d in steps]
    y_peers = [at(y=turn(y, d)) for d in steps]
    skew = 2 - 4 * lax.rem(zl, 2)
    z_peers = [at_z(turn(z, 1, 16)), at_z(turn(z, -1, 16)), at_z(turn(z, skew, 16))]
    z_from = (turn(zl, -1), turn(zl, 1), turn(zl, 2))
    flips = (3 - zl, turn(zl, 2), zl + 1 - 2 * lax.rem(zl, 2), zl)
    middle = (zl * (3 - zl)) // 2

    loads = []
    for i, (src, dst) in enumerate((
        (lf_h, lf), (acts_h, acts), (gain_h, gain),
        (cot_h, cot.at[pl.ds(pl.multiple_of(y * 128, 128), 128)]),
        (g_h, g), (m_h, m), (w_h, w), (fm_h, fm), (sm_h, sm),
    )):
        copy = pltpu.make_async_copy(src, dst, load_sem.at[i])
        copy.start()
        loads.append(copy)

    barrier = pltpu.get_barrier_semaphore()
    near = [other] + x_peers + y_peers
    near += [at(zl=flips[s]) for s in range(3)]
    near += [at_z(turn(z, d, 16)) for d in (1, -1, 2, -2)]
    for device in near:
        signal(barrier, device)

    loads[0].wait()
    for k in range(4):
        turned = lf[:, k * 128:(k + 1) * 128].T
        for j in range(4):
            lt[j, k] = turned[j * 32:(j + 1) * 32]
    loads[3].wait()

    pl.semaphore_wait(barrier, len(near))

    far = [turn(zh, d) for d in (2, 1, 3, 0)]
    along = []
    for k in range(4):
        along.append([
            send(lt.at[turn(x, d), far[k]], lr.at[i, k], along_s.at[k * 3 + i], along_r.at[k * 3 + i], x_peers[i])
            for i, d in enumerate(steps)
        ])
    mine = pl.ds(pl.multiple_of(y * 128, 128), 128)
    cots = [send(cot.at[mine], cot.at[mine], cot_s.at[i], cot_r.at[i], y_peers[i]) for i in range(3)]
    for d in (2, -2):
        signal(vouch.at[0], at_z(turn(z, d, 16)))

    loads[1].wait()
    loads[2].wait()

    def norm_rows(i, carry):
        rows = pl.ds(pl.multiple_of(i * 16, 16), 16)
        full = acts[rows, :].astype(F32)
        rstd = lax.rsqrt(jnp.sum(full * full, axis=1, keepdims=True) / 8192.0 + norm_epsilon)
        normed[rows, :] = (full * rstd * gain[...]).astype(BF16)
        return carry

    lax.fori_loop(0, 4, norm_rows, 0)
    pl.semaphore_wait(vouch.at[0], 2)
    for d in (4, -4):
        signal(vouch.at[1], at_z(turn(z, d, 16)))
    lax.fori_loop(4, 8, norm_rows, 0)

    chunks, keeps = [], []
    for s in range(4):
        row = []
        for i, d in enumerate(steps):
            cols = pl.ds(pl.multiple_of(turn(y, d) * 2048 + flips[s] * 512, 512), 512)
            row.append(send(normed.at[:, cols], xs.at[s, mine], tok_s.at[s * 3 + i], tok_r.at[s * 3 + i], y_peers[i]))
        cols = pl.ds(pl.multiple_of(y * 2048 + flips[s] * 512, 512), 512)
        keep = pltpu.make_async_copy(normed.at[:, cols], xs.at[s, mine], keep_sem.at[s])
        keep.start()
        keeps.append(keep)
        chunks.append(row)

    def sum_along(k):
        for copy in along[k]:
            copy.wait_recv()
        part[k] = lt[x, far[k]] + lr[0, k] + lr[1, k] + lr[2, k]
        if k == 0:
            pl.semaphore_wait(vouch.at[1], 2)
        if k < 3:
            return send(part.at[k], pr.at[k], far_s.at[k], far_r.at[k], at(zh=far[k]))

    def outer_update(copies):
        for copy in copies:
            copy.wait_recv()
        loads[4].wait()
        loads[5].wait()
        total = part[3] + pr[0] + pr[1] + pr[2]
        mean_delta = g[...] - total / 16.0
        new_momentum = outer_beta * m[...] + mean_delta
        new_global = g[...] - outer_rate * (mean_delta + outer_beta * new_momentum)
        ng_o[...] = new_global
        nm_o[...] = new_momentum
        nt[zl, c, zh, x] = new_global.astype(BF16)
        piece = nt.at[zl, c, zh, x]
        return [send(piece, piece, gat_s.at[k], gat_r.at[k], at(zh=far[k])) for k in range(3)]

    def columns(h):
        return pl.ds(2 * h, 2)

    def gather_z(copies):
        for copy in copies:
            copy.wait_recv()
        line, wide = [], [[], []]
        for h in range(2):
            piece = nt.at[zl, c, columns(h), x]
            for i in range(3):
                line.append(send(piece, piece, line_s.at[h * 3 + i], line_r.at[h * 3 + i], z_peers[i]))
        for h in range(2):
            piece = nt.at[zl, c, columns(h), x]
            for i in range(3):
                wide[h].append(send(piece, piece, wide_s.at[h * 12 + i], wide_r.at[h * 12 + i], x_peers[i]))
        return line, wide

    def gather_x(line, wide):
        for h in range(2):
            for j in range(3):
                line[h * 3 + j].wait_recv()
                piece = nt.at[z_from[j], c, columns(h), x]
                for i in range(3):
                    n = h * 12 + 3 + j * 3 + i
                    wide[h].append(send(piece, piece, wide_s.at[n], wide_r.at[n], x_peers[i]))

    def gather_core(wide, h):
        for copy in wide[h]:
            copy.wait_recv()
        piece = nt.at[:, c, columns(h)]
        return send(piece, piece, core_s.at[h], core_r.at[h], other)

    def half(core):
        return pl.ds(pl.multiple_of(core * 256, 256), 256)

    def grad_of(s, core):
        return lax.dot_general(
            xs[s, :, half(core)], cot[...], (((0,), (0,)), ((), ())), preferred_element_type=F32
        )

    def chunk_in(s):
        for copy in chunks[s]:
            copy.wait_recv()
        keeps[s].wait()
        gsend[s] = grad_of(s, 1 - c)
        copy = send(gsend.at[s], grecv.at[s], grad_s.at[s], grad_r.at[s], other)
        gown[s] = grad_of(s, c)
        return copy

    def arrived(slot):
        pltpu.make_async_remote_copy(
            src_ref=zsend.at[0], dst_ref=zrecv.at[slot], send_sem=z_s.at[0], recv_sem=z_r.at[slot],
            device_id=other, device_id_type=MESH,
        ).wait_recv()

    def chunk_out(s, copy):
        copy.wait_recv()
        total = gown[s] + grecv[s]
        if s == 0:
            zsend[s] = total.astype(BF16)
            slot = 3 * (1 - middle)
            owner = middle * flips[0] + (1 - middle) * flips[2]
            return send(zsend.at[s], zrecv.at[slot], z_s.at[s], z_r.at[slot], at(zl=owner))
        if s == 1:
            gown[s] = total

            @pl.when(middle == 1)
            def _():
                arrived(3)
                gown[s] = gown[s] + zrecv[3].astype(F32)

            total = gown[s]
        zsend[s] = total.astype(BF16)
        return send(zsend.at[s], zrecv.at[s], z_s.at[s], z_r.at[s], at(zl=flips[s]))

    def features(h):
        total = None
        for s in range(4):
            for core in range(2):
                rows = nt[flips[s], core, 2 * h:2 * h + 2].reshape(256, 256)
                term = lax.dot_general(
                    xs[s, :, core * 256:(core + 1) * 256], rows,
                    (((1,), (1,)), ((), ())), preferred_element_type=F32,
                )
                total = term if total is None else total + term
        for k in range(4):
            fown[h, k] = total[k * 128:(k + 1) * 128]
        out = []
        for i, d in enumerate(steps):
            fsend[h, i] = fown[h, turn(y, d)].astype(BF16)
            n = h * 3 + i
            out.append(send(fsend.at[h, i], frecv.at[h, i], feat_s.at[n], feat_r.at[n], y_peers[i]))
        return out

    far_copies = [sum_along(k) for k in range(4)][:3]
    for copy in cots:
        copy.wait_recv()
    gat_copies = outer_update(far_copies)
    g0 = chunk_in(0)
    line, wide = gather_z(gat_copies)
    chunk_out(0, g0)
    gather_x(line, wide)
    g1 = chunk_in(1)
    chunk_out(1, g1)
    g2 = chunk_in(2)
    core0 = gather_core(wide, 0)
    chunk_out(2, g2)
    core1 = gather_core(wide, 1)
    g3 = chunk_in(3)
    core0.wait_recv()
    feats = [features(0)]
    core1.wait_recv()
    feats.append(features(1))

    g3.wait_recv()
    for i in (6, 7, 8):
        loads[i].wait()
    arrived(1)
    arrived(2)
    gown[3] = gown[3] + grecv[3] + zrecv[1].astype(F32) + zrecv[2].astype(F32)

    @pl.when(middle == 1)
    def _():
        arrived(0)
        gown[3] = gown[3] + zrecv[0].astype(F32)

    grad = gown[3]
    first = beta_one * fm[...].astype(F32) + (1.0 - beta_one) * grad
    second = beta_two * sm[...].astype(F32) + (1.0 - beta_two) * grad * grad
    ratio = first / bias_first / (jnp.sqrt(second / bias_second) + adam_epsilon)
    w_o[...] = w[...] - inner_rate * (ratio + weight_decay * w[...])
    fm_o[...] = first.astype(BF16)
    sm_o[...] = second.astype(BF16)

    for h in range(2):
        for copy in feats[h]:
            copy.wait_recv()
        total = fown[h, y] + frecv[h, 0].astype(F32) + frecv[h, 1].astype(F32) + frecv[h, 2].astype(F32)
        ft_o[:, h * 256:(h + 1) * 256] = total.astype(BF16)

    for copy in sends:
        copy.wait_send()


def hand_over(*refs):
    for i in range(6):
        refs[6 + i][...] = refs[i][...]


def body(
    acts,
    norm_gain,
    cotangent,
    inner_weight,
    first_moment,
    second_moment,
    local_fragment,
    global_fragment,
    outer_momentum,
):
    vmem, anywhere = pl.BlockSpec(memory_space=pltpu.VMEM), pl.BlockSpec(memory_space=pl.ANY)
    dma = pltpu.SemaphoreType.DMA
    outs = pl.pallas_call(
        kernel,
        out_shape=(
            jax.ShapeDtypeStruct((256, 512), F32),
            jax.ShapeDtypeStruct((256, 512), BF16),
            jax.ShapeDtypeStruct((256, 512), BF16),
            jax.ShapeDtypeStruct((32, 256), F32),
            jax.ShapeDtypeStruct((32, 256), F32),
            jax.ShapeDtypeStruct((128, 512), BF16),
        ),
        in_specs=[anywhere] * 9,
        out_specs=[vmem] * 6,
        scratch_shapes=[
            pltpu.VMEM((128, 8192), BF16),
            pltpu.VMEM((1, 8192), F32),
            pltpu.VMEM((128, 8192), BF16),
            pltpu.VMEM((512, 512), BF16),
            pltpu.VMEM((256, 512), F32),
            pltpu.VMEM((256, 512), BF16),
            pltpu.VMEM((256, 512), BF16),
            pltpu.VMEM((256, 512), F32),
            pltpu.VMEM((32, 256), F32),
            pltpu.VMEM((32, 256), F32),
            pltpu.VMEM((4, 4, 32, 256), F32),
            pltpu.VMEM((3, 4, 32, 256), F32),
            pltpu.VMEM((4, 32, 256), F32),
            pltpu.VMEM((3, 32, 256), F32),
            pltpu.VMEM((4, 2, 4, 4, 32, 256), BF16),
            pltpu.VMEM((4, 512, 512), BF16),
            pltpu.VMEM((4, 256, 512), F32),
            pltpu.VMEM((4, 256, 512), F32),
            pltpu.VMEM((4, 256, 512), F32),
            pltpu.VMEM((3, 256, 512), BF16),
            pltpu.VMEM((4, 256, 512), BF16),
            pltpu.VMEM((2, 4, 128, 256), F32),
            pltpu.VMEM((2, 3, 128, 256), BF16),
            pltpu.VMEM((2, 3, 128, 256), BF16),
            dma((9,)), dma((4,)), pltpu.SemaphoreType.REGULAR((2,)),
        ] + [
            dma((n,)) for n in (3, 12, 12, 3, 3, 6, 24, 2, 4, 4, 6) for _ in range(2)
        ],
        compiler_params=pltpu.CompilerParams(
            collective_id=0, has_side_effects=True, vmem_limit_bytes=63 * 2**20
        ),
        name="window_step",
    )(
        acts, norm_gain[None], cotangent, inner_weight[0], first_moment[0], second_moment[0],
        local_fragment[0], global_fragment.T, outer_momentum.T,
    )
    outs = pl.pallas_call(
        hand_over,
        out_shape=[jax.ShapeDtypeStruct(out.shape, out.dtype) for out in outs],
        in_specs=[vmem] * 6,
        out_specs=[vmem] * 6,
        name="finish",
    )(*outs)
    new_weight, new_first, new_second, new_global, new_momentum, features = outs
    return (new_weight[None], new_first[None], new_second[None], new_global.T, new_momentum.T, features)


def solution(mesh):
    placed = (
        P(("replica", "fsdp"), None),
        P(),
        P(("replica", "fsdp"), None),
        P("replica", "fsdp", None),
        P("replica", "fsdp", None),
        P("replica", "fsdp", None),
        P("replica", "fsdp", None),
        P("fsdp", "replica"),
        P("fsdp", "replica"),
    )
    return jax.shard_map(
        body,
        mesh=mesh,
        in_specs=placed,
        out_specs=(
            P("replica", "fsdp", None),
            P("replica", "fsdp", None),
            P("replica", "fsdp", None),
            P("fsdp", "replica"),
            P("fsdp", "replica"),
            P(("replica", "fsdp"), None),
        ),
        check_vma=False,
    )
```

time: 87.1 us -> 63 us (0.72)
  the two profiles are of different devices: /device:TPU:33 before, /device:TPU:24 now
where the time goes in v2:
time: 63 us; the launch traced here: 62.5 us
  Pallas kernels  61.9 us (98%)
  between operations  0.64 us (1%)
    pallas_call x1, Pallas kernels, body(): pl.pallas_call(kernel, out_shape=(jax.ShapeDtypeStruct((256, 512), F32),...  59.6 us
    pallas_call x1, Pallas kernels, body(): pl.pallas_call(hand_over, out_shape=[jax.ShapeDtypeStruct(out.shape, out....  2.3 us

profile of v2, /device:TPU:24, one launch (start us, length us, event | category | flops | bytes accessed | tf_op | source)
XLA Modules:
  0.0 62.5 jit_solution(13072609724939395930)
XLA Ops:
  0.6 59.6 %window_step.1 = (f32[256,512]{1,0:T(8,128)}, bf16[256,512]{1,0:T(8,128)(2,1)}, bf16[256,512]{1,0:T(8,128)(2,1)}, f32[32,256]{1,0:T(8,128)}, f32[32,256]{1,0:T(8,128)}, /*index=5*/bf16[128,512]{1,0:T(8,128)(2,1)}) custom-call(bf16[128,8192]{1,0:T(8,128)(2,1)} %acts_h.1, f32[1,8192]{1,0:T(1,128)} %bitcast.16, bf16[128,512]{1,0:T(8,128)(2,1)} %cot_h.1, ...), custom_call_target="tpu_custom_call" | custom-call | tf_op jit(solution)/shard_map/window_step/pallas_call | solution.py:327
  60.2 2.3 %finish.1 = (f32[256,512]{1,0:T(8,128)}, bf16[256,512]{1,0:T(8,128)(2,1)}, bf16[256,512]{1,0:T(8,128)(2,1)}, f32[32,256]{1,0:T(8,128)}, f32[32,256]{1,0:T(8,128)}, /*index=5*/bf16[128,512]{1,0:T(8,128)(2,1)}) custom-call(f32[256,512]{1,0:T(8,128)} %get-tuple-element.18.refs_0_, bf16[256,512]{1,0:T(8,128)(2,1)} %get-tuple-element.19.refs_1_, ...), custom_call_target="tpu_custom_call" | custom-call | tf_op jit(solution)/shard_map/finish/pallas_call | solution.py:376

commit v3 on v2

v3 whole, which is shorter than its diff:
```python
import functools

import jax
import jax.numpy as jnp
from jax import lax
from jax.experimental import pallas as pl
from jax.experimental.pallas import tpu as pltpu
from jax.sharding import PartitionSpec as P

beta_one = 0.9
beta_two = 0.95
adam_epsilon = 1e-08
inner_rate = 0.01
weight_decay = 0.1
bias_first = 1.0 - 0.9**20
bias_second = 1.0 - 0.95**20
outer_rate = 0.7
outer_beta = 0.9
norm_epsilon = 1e-05

MESH = pl.DeviceIdType.MESH
F32 = jnp.float32
BF16 = jnp.bfloat16


def kernel(
    acts_h, gain_h, cot_h, w_h, fm_h, sm_h, lf_h, g_h, m_h,
    w_o, fm_o, sm_o, ng_o, nm_o, ft_o,
    acts, gain, normed, cot, w, fm, sm, lf, g, m,
    lt, lr, part, pr, nt, xs, gown, zsend, zrecv, fpart, fcore, fown, fsend, frecv,
    load_sem, keep_sem, vouch,
    cot_s, cot_r, tok_s, tok_r, along_s, along_r, far_s, far_r, gat_s, gat_r,
    line_s, line_r, wide_s, wide_r, core_s, core_r,
    z_s, z_r, feat_s, feat_r,
):
    rep = lax.axis_index("replica")
    fs = lax.axis_index("fsdp")
    zh, x = rep // 4, lax.rem(rep, 4)
    y, zl, c = fs // 8, lax.rem(fs // 2, 4), lax.rem(fs, 2)
    z = zh * 4 + zl

    def at(zh=zh, x=x, y=y, zl=zl, c=c):
        return (zh * 4 + x, y * 8 + zl * 2 + c)

    def at_z(zz):
        return at(zh=zz // 4, zl=lax.rem(zz, 4))

    def turn(value, step, size=4):
        return lax.rem(value + step + size, size)

    sends = []

    def send(src, dst, ss, rs, device):
        copy = pltpu.make_async_remote_copy(
            src_ref=src, dst_ref=dst, send_sem=ss, recv_sem=rs,
            device_id=device, device_id_type=MESH,
        )
        copy.start()
        sends.append(copy)
        return copy

    def signal(sem, device):
        pl.semaphore_signal(sem, inc=1, device_id=device, device_id_type=MESH)

    other = at(c=1 - c)
    steps = (1, 3, 2)
    x_peers = [at(x=turn(x, d)) for d in steps]
    y_peers = [at(y=turn(y, d)) for d in steps]
    flips = (3 - zl, turn(zl, 2), zl + 1 - 2 * lax.rem(zl, 2), zl)
    middle = (zl * (3 - zl)) // 2
    line_peers = [at(zl=flips[s]) for s in range(3)]
    skew = 2 - 4 * lax.rem(zl, 2)
    z_peers = [at_z(turn(z, 1, 16)), at_z(turn(z, -1, 16)), at_z(turn(z, skew, 16))]
    z_from = (turn(zl, -1), turn(zl, 1), turn(zl, 2))
    mine = pl.ds(pl.multiple_of(c * 512 + y * 128, 128), 128)
    takers = [(turn(y, d), core) for d in steps for core in (c, 1 - c)] + [(y, 1 - c)]

    loads = []
    for i, (src, dst) in enumerate((
        (lf_h, lf), (acts_h, acts), (gain_h, gain),
        (cot_h, cot.at[mine]),
        (g_h, g), (m_h, m), (w_h, w), (fm_h, fm), (sm_h, sm),
    )):
        copy = pltpu.make_async_copy(src, dst, load_sem.at[i])
        copy.start()
        loads.append(copy)

    barrier = pltpu.get_barrier_semaphore()
    near = [other] + x_peers + y_peers
    near += line_peers + [at(y=turn(y, d), c=1 - c) for d in steps]
    near += [at_z(turn(z, d, 16)) for d in (1, -1, 2, -2)]
    for device in near:
        signal(barrier, device)

    loads[0].wait()
    for k in range(4):
        turned = lf[:, k * 128:(k + 1) * 128].T
        for j in range(4):
            lt[j, k] = turned[j * 32:(j + 1) * 32]
    loads[3].wait()

    pl.semaphore_wait(barrier, len(near))

    for d in (2, -2):
        signal(vouch.at[0], at_z(turn(z, d, 16)))
    far = [turn(zh, d) for d in (2, 1, 3, 0)]
    along = []
    for k in range(4):
        along.append([
            send(lt.at[turn(x, d), far[k]], lr.at[i, k], along_s.at[k * 3 + i], along_r.at[k * 3 + i], x_peers[i])
            for i, d in enumerate(steps)
        ])
    cots = [send(cot.at[mine], cot.at[mine], cot_s.at[i], cot_r.at[i], y_peers[i]) for i in range(3)]
    loads[1].wait()
    loads[2].wait()

    def norm_rows(i, carry):
        rows = pl.ds(pl.multiple_of(i * 16, 16), 16)
        full = acts[rows, :].astype(F32)
        rstd = lax.rsqrt(jnp.sum(full * full, axis=1, keepdims=True) / 8192.0 + norm_epsilon)
        normed[rows, :] = (full * rstd * gain[...]).astype(BF16)
        return carry

    pl.semaphore_wait(vouch.at[0], 2)
    for d in (4, -4):
        signal(vouch.at[1], at_z(turn(z, d, 16)))
    lax.fori_loop(0, 8, norm_rows, 0)

    def columns_of(yy, s, core):
        return pl.ds(pl.multiple_of(yy * 2048 + flips[s] * 512 + core * 256, 256), 256)

    for s in range(4):
        pltpu.make_async_copy(normed.at[:, columns_of(y, s, c)], xs.at[s, mine], keep_sem.at[s]).start()
        for n, (yy, core) in enumerate(takers):
            send(
                normed.at[:, columns_of(yy, s, core)], xs.at[s, mine],
                tok_s.at[s * 7 + n], tok_r.at[s * 7 + n], at(y=yy, c=core),
            )

    def landed(ref, sem):
        pltpu.make_async_remote_copy(
            src_ref=ref, dst_ref=ref, send_sem=z_s.at[0], recv_sem=sem,
            device_id=other, device_id_type=MESH,
        ).wait_recv()

    def sum_along(k):
        for copy in along[k]:
            copy.wait_recv()
        part[k] = lt[x, far[k]] + lr[0, k] + lr[1, k] + lr[2, k]
        if k == 0:
            pl.semaphore_wait(vouch.at[1], 2)
        if k < 3:
            send(part.at[k], pr.at[k], far_s.at[k], far_r.at[k], at(zh=far[k]))

    def cot_to_core():
        for copy in cots:
            copy.wait_recv()
        whole = cot.at[pl.ds(pl.multiple_of(c * 512, 512), 512)]
        send(whole, whole, cot_s.at[3], cot_r.at[3], other)

    def outer_update():
        for k in range(3):
            landed(pr.at[k], far_r.at[k])
        loads[4].wait()
        loads[5].wait()
        total = part[3] + pr[0] + pr[1] + pr[2]
        mean_delta = g[...] - total / 16.0
        new_momentum = outer_beta * m[...] + mean_delta
        new_global = g[...] - outer_rate * (mean_delta + outer_beta * new_momentum)
        ng_o[...] = new_global
        nm_o[...] = new_momentum
        nt[zl, zh, x] = new_global.astype(BF16)
        piece = nt.at[zl, zh, x]
        for k in range(3):
            send(piece, piece, gat_s.at[k], gat_r.at[k], at(zh=far[k]))

    def gather_z():
        for k in range(3):
            landed(nt.at[zl, far[k], x], gat_r.at[k])
        for h in range(2):
            piece = nt.at[zl, pl.ds(2 * h, 2), x]
            for i in range(3):
                send(piece, piece, line_s.at[h * 3 + i], line_r.at[h * 3 + i], z_peers[i])
        for h in range(2):
            piece = nt.at[zl, pl.ds(2 * h, 2), x]
            for i in range(3):
                send(piece, piece, wide_s.at[h * 12 + i], wide_r.at[h * 12 + i], x_peers[i])

    def gather_x(h):
        for j in range(3):
            piece = nt.at[z_from[j], pl.ds(2 * h, 2), x]
            landed(piece, line_r.at[h * 3 + j])
            for i in range(3):
                n = h * 12 + 3 + j * 3 + i
                send(piece, piece, wide_s.at[n], wide_r.at[n], x_peers[i])

    def grads(s):
        if s == 0:
            landed(cot.at[pl.ds(pl.multiple_of(512 - c * 512, 512), 512)], cot_r.at[3])
        for n in range(7):
            landed(xs.at[s, mine], tok_r.at[s * 7 + n])
        pltpu.make_async_copy(normed.at[:, pl.ds(0, 256)], xs.at[s, mine], keep_sem.at[s]).wait()
        total = lax.dot_general(
            xs[s], cot[...], (((0,), (0,)), ((), ())), preferred_element_type=F32
        )
        if s == 0:
            zsend[s] = total.astype(BF16)
            slot = 3 * (1 - middle)
            owner = middle * flips[0] + (1 - middle) * flips[2]
            send(zsend.at[s], zrecv.at[slot], z_s.at[s], z_r.at[slot], at(zl=owner))
            return
        if s == 3:
            gown[...] = total
            return
        if s == 1:
            gown[...] = total

            @pl.when(middle == 1)
            def _():
                landed(zrecv.at[3], z_r.at[3])
                gown[...] = gown[...] + zrecv[3].astype(F32)

            total = gown[...]
        zsend[s] = total.astype(BF16)
        send(zsend.at[s], zrecv.at[s], z_s.at[s], z_r.at[s], line_peers[s])

    def features(h):
        for j in range(4):
            for i, d in enumerate(steps):
                piece = nt.at[zl if j == 0 else z_from[j - 1], pl.ds(2 * h, 2), turn(x, -d)]
                landed(piece, wide_r.at[h * 12 + j * 3 + i])
        total = None
        for s in range(4):
            rows = nt[flips[s], 2 * h:2 * h + 2].reshape(256, 256)
            term = lax.dot_general(
                xs[s], rows, (((1,), (1,)), ((), ())), preferred_element_type=F32
            )
            total = term if total is None else total + term
        for k in range(8):
            fpart[h, k // 4, k % 4] = total[k * 128:(k + 1) * 128]
        fcore[h, 0] = fpart[h, 1 - c].astype(BF16)
        send(fcore.at[h, 0], fcore.at[h, 1], core_s.at[h], core_r.at[h], other)

    def features_along(h):
        landed(fcore.at[h, 1], core_r.at[h])
        fown[h] = fpart[h, c] + fcore[h, 1].astype(F32)
        for i, d in enumerate(steps):
            fsend[h, i] = fown[h, turn(y, d)].astype(BF16)
            n = h * 3 + i
            send(fsend.at[h, i], frecv.at[h, i], feat_s.at[n], feat_r.at[n], y_peers[i])

    def inner_update():
        for i in (6, 7, 8):
            loads[i].wait()
        landed(zrecv.at[1], z_r.at[1])
        landed(zrecv.at[2], z_r.at[2])
        gown[...] = gown[...] + zrecv[1].astype(F32) + zrecv[2].astype(F32)

        @pl.when(middle == 1)
        def _():
            landed(zrecv.at[0], z_r.at[0])
            gown[...] = gown[...] + zrecv[0].astype(F32)

        grad = gown[...]
        first = beta_one * fm[...].astype(F32) + (1.0 - beta_one) * grad
        second = beta_two * sm[...].astype(F32) + (1.0 - beta_two) * grad * grad
        ratio = first / bias_first / (jnp.sqrt(second / bias_second) + adam_epsilon)
        w_o[...] = w[...] - inner_rate * (ratio + weight_decay * w[...])
        fm_o[...] = first.astype(BF16)
        sm_o[...] = second.astype(BF16)

    def features_out(h):
        total = fown[h, y]
        for i in range(3):
            landed(frecv.at[h, i], feat_r.at[h * 3 + i])
            total = total + frecv[h, i].astype(F32)
        ft_o[:, h * 256:(h + 1) * 256] = total.astype(BF16)

    for k in range(4):
        sum_along(k)
    cot_to_core()
    outer_update()
    grads(0)
    gather_z()
    gather_x(0)
    gather_x(1)
    grads(1)
    grads(2)
    grads(3)
    features(0)
    features_along(0)
    features(1)
    features_along(1)
    inner_update()
    features_out(0)
    features_out(1)

    for copy in sends:
        copy.wait_send()


def hand_over(*refs):
    copies = []
    for i in range(6):
        copy = pltpu.make_async_copy(refs[i], refs[6 + i], refs[12].at[i])
        copy.start()
        copies.append(copy)
    for copy in copies:
        copy.wait()


def body(
    acts,
    norm_gain,
    cotangent,
    inner_weight,
    first_moment,
    second_moment,
    local_fragment,
    global_fragment,
    outer_momentum,
):
    vmem, anywhere = pl.BlockSpec(memory_space=pltpu.VMEM), pl.BlockSpec(memory_space=pl.ANY)
    dma = pltpu.SemaphoreType.DMA
    outs = pl.pallas_call(
        kernel,
        out_shape=(
            pltpu.VMEM((256, 512), F32),
            pltpu.VMEM((256, 512), BF16),
            pltpu.VMEM((256, 512), BF16),
            pltpu.VMEM((32, 256), F32),
            pltpu.VMEM((32, 256), F32),
            pltpu.VMEM((128, 512), BF16),
        ),
        in_specs=[anywhere] * 9,
        out_specs=[vmem] * 6,
        scratch_shapes=[
            pltpu.VMEM((128, 8192), BF16),
            pltpu.VMEM((1, 8192), F32),
            pltpu.VMEM((128, 8192), BF16),
            pltpu.VMEM((1024, 512), BF16),
            pltpu.VMEM((256, 512), F32),
            pltpu.VMEM((256, 512), BF16),
            pltpu.VMEM((256, 512), BF16),
            pltpu.VMEM((256, 512), F32),
            pltpu.VMEM((32, 256), F32),
            pltpu.VMEM((32, 256), F32),
            pltpu.VMEM((4, 4, 32, 256), F32),
            pltpu.VMEM((3, 4, 32, 256), F32),
            pltpu.VMEM((4, 32, 256), F32),
            pltpu.VMEM((3, 32, 256), F32),
            pltpu.VMEM((4, 4, 4, 32, 256), BF16),
            pltpu.VMEM((4, 1024, 256), BF16),
            pltpu.VMEM((256, 512), F32),
            pltpu.VMEM((3, 256, 512), BF16),
            pltpu.VMEM((4, 256, 512), BF16),
            pltpu.VMEM((2, 2, 4, 128, 256), F32),
            pltpu.VMEM((2, 2, 4, 128, 256), BF16),
            pltpu.VMEM((2, 4, 128, 256), F32),
            pltpu.VMEM((2, 3, 128, 256), BF16),
            pltpu.VMEM((2, 3, 128, 256), BF16),
            dma((9,)), dma((4,)), pltpu.SemaphoreType.REGULAR((2,)),
        ] + [
            dma((n,)) for n in (4, 28, 12, 3, 3, 6, 24, 2, 4, 6) for _ in range(2)
        ],
        compiler_params=pltpu.CompilerParams(
            collective_id=0, has_side_effects=True, vmem_limit_bytes=60 * 2**20
        ),
        name="window_step",
    )(
        acts, norm_gain[None], cotangent, inner_weight[0], first_moment[0], second_moment[0],
        local_fragment[0], global_fragment.T, outer_momentum.T,
    )
    outs = pl.pallas_call(
        hand_over,
        out_shape=[jax.ShapeDtypeStruct(out.shape, out.dtype) for out in outs],
        in_specs=[anywhere] * 6,
        out_specs=[anywhere] * 6,
        scratch_shapes=[dma((6,))],
        name="finish",
    )(*[pltpu.with_memory_space_constraint(out, pltpu.VMEM) for out in outs])
    new_weight, new_first, new_second, new_global, new_momentum, features = outs
    return (new_weight[None], new_first[None], new_second[None], new_global.T, new_momentum.T, features)


def solution(mesh):
    placed = (
        P(("replica", "fsdp"), None),
        P(),
        P(("replica", "fsdp"), None),
        P("replica", "fsdp", None),
        P("replica", "fsdp", None),
        P("replica", "fsdp", None),
        P("replica", "fsdp", None),
        P("fsdp", "replica"),
        P("fsdp", "replica"),
    )
    return jax.shard_map(
        body,
        mesh=mesh,
        in_specs=placed,
        out_specs=(
            P("replica", "fsdp", None),
            P("replica", "fsdp", None),
            P("replica", "fsdp", None),
            P("fsdp", "replica"),
            P("fsdp", "replica"),
            P(("replica", "fsdp"), None),
        ),
        check_vma=False,
    )
```

time: 63 us -> 60.3 us (0.957)
  Pallas kernels: 61.9 us -> 59.5 us
    pallas_call x1, Pallas kernels: 2.3 us -> 1.08 us  [body(): pl.pallas_call(hand_over, out_shape=[jax.ShapeDtypeStruct(out.shape, out....]
    pallas_call x1, Pallas kernels: 59.6 us -> 58.5 us  [body(): pl.pallas_call(kernel, out_shape=(pltpu.VMEM((256, 512), F32), pltpu.VMEM...]
where the time goes in v3:
time: 60.3 us; the launch traced here: 60.2 us
  Pallas kernels  59.5 us (99%)
  between operations  0.64 us (1%)
    pallas_call x1, Pallas kernels, body(): pl.pallas_call(kernel, out_shape=(pltpu.VMEM((256, 512), F32), pltpu.VMEM...  58.5 us

profile of v3, /device:TPU:24, one launch (start us, length us, event | category | flops | bytes accessed | tf_op | source)
XLA Modules:
  0.0 60.2 jit_solution(12664956812217911449)
XLA Ops:
  0.6 58.5 %window_step.1 = (f32[256,512]{1,0:T(8,128)S(1)}, bf16[256,512]{1,0:T(8,128)(2,1)S(1)}, bf16[256,512]{1,0:T(8,128)(2,1)S(1)}, f32[32,256]{1,0:T(8,128)S(1)}, f32...) custom-call(bf16[128,8192]{1,0:T(8,128)(2,1)} %acts_h.1, f32[1,8192]{1,0:T(1,128)} %bitcast.16, bf16[128,512]{1,0:T(8,128)(2,1)} %cot_h.1, ...), custom_call_target="tpu_custom_call" | custom-call | tf_op jit(solution)/shard_map/window_step/pallas_call | solution.py:325
  59.1 1.1 %finish.1 = (f32[256,512]{1,0:T(8,128)}, bf16[256,512]{1,0:T(8,128)(2,1)}, bf16[256,512]{1,0:T(8,128)(2,1)}, f32[32,256]{1,0:T(8,128)}, f32[32,256]{1,0:T(8,128)}, /*index=5*/bf16[128,512]{1,0:T(8,128)(2,1)}) custom-call(f32[256,512]{1,0:T(8,128)S(1)} %get-tuple-element.18.refs_0_, bf16[256,512]{1,0:T(8,128)(2,1)S(1)} %get-tuple-element.19.refs_1_, ...), custom_call_target="tpu_custom_call" | custom-call | tf_op jit(solution)/shard_map/finish/pallas_call | solution.py:374
